TPU v7x, 512 devices: a whole 4x4x16 slice. The times are simulated.
512 devices in a mesh: seg: 8 (over x, core), sec: 64 (over z, y).
Axes of the slice: x: 4, y: 4, z: 16, core: 2. Of those that a mesh axis runs over, the one named last changes fastest.
Arguments:
- psi: float32 [8, 8192, 256], P('seg', 'sec'), may hold values from -36 to 36
- left_env: bfloat16 [8, 26, 8192, 128], P('seg', None, 'sec'), may hold values from -3 to 3
- right_env: bfloat16 [8, 26, 256, 256], P('seg'), may hold values from -3 to 3
- term_kind: int32 [26], replicated, may hold values from 0 to 4, as said below
- block_rows: int32 [8, 64], P('seg', 'sec'), may hold values from 16 to 128, as said below
Outputs:
- updated: float32 [8, 8192, 256], P('seg', 'sec')
Inputs may be any that keep to these rules, and one draw needn't show every extreme that they name: `term_kind`: each of the five kinds is taken by some MPO index. `block_rows`: in every segment one block is full and one has 16 live rows.
All inputs are finite; a program needn't handle non-finite values.
Results may differ from a plain program's by a relative error of at most 0.01.
Values may be sent and summed in bfloat16 or wider, within the bound.
A program may use at most 64 MiB of HBM per device.

v0:
```python
import jax
import jax.numpy as jnp
from jax import lax
from jax.sharding import PartitionSpec as P

NDN = 8
KRYLOV = 3


eps = 1e-06
series_order = 3
step_size = 0.5


def shifted(shard, axis, by):
    count = lax.axis_size(axis)
    pairs = [(i, i + by) for i in range(count) if 0 <= i + by < count]
    return lax.ppermute(shard, axis, pairs)


def tridiag_coeffs(alphas, betas):
    count = len(alphas)
    diag_part = jnp.diag(jnp.stack(alphas))
    off_part = jnp.diag(jnp.stack(betas), 1) + jnp.diag(jnp.stack(betas), -1)
    matrix = (diag_part + off_part).astype(jnp.float32)
    term = jnp.zeros((count,), jnp.float32).at[0].set(1.0)
    total = term
    for order in range(1, series_order + 1):
        term = jnp.sum(matrix * term[None, :], axis=1) * (-step_size / order)
        total = total + term
    return total


def inner(first, second):
    return jnp.sum(first * second)


def boundary_env(first_bf, right):
    scale = (first_bf.shape[1] * first_bf.shape[0] * right.shape[0]) ** (-0.5)
    projected = jnp.einsum(
        "bc,wcd->wbd", first_bf, right, preferred_element_type=jnp.float32
    ).astype(jnp.bfloat16)
    env = jnp.einsum("wbd,ed->wbe", projected, first_bf, preferred_element_type=jnp.float32) * scale
    return env.astype(jnp.bfloat16)


def per_device(psi, left_env, right_env, term_kind, block_rows):
    blk = psi.shape[1]
    cols = psi.shape[2]
    count = 1.0 * lax.axis_size("sec") * blk * cols
    live = (lax.iota(jnp.int32, blk) < block_rows[0, 0]).astype(jnp.float32)[:, None]
    place = lax.axis_index("sec")
    keep_upper = place % NDN != NDN - 1
    keep_lower = place % NDN != 0
    onehot = (term_kind[:, None] == lax.iota(jnp.int32, 5)[None, :]).astype(jnp.bfloat16)
    right = right_env[0]
    left = left_env[0]

    def apply_op(left_blocks, vec):
        vec_bf = vec.astype(jnp.bfloat16)
        pieces = [vec_bf]
        for offset in (-1, 1, -NDN, NDN):
            pieces.append(shifted(vec_bf, "sec", offset))
        pieces[1] = jnp.where(keep_upper, pieces[1], jnp.zeros_like(vec_bf))
        pieces[2] = jnp.where(keep_lower, pieces[2], jnp.zeros_like(vec_bf))
        stacked = jnp.stack(pieces)
        chosen = jnp.einsum(
            "wk,kbc->wbc", onehot, stacked, preferred_element_type=jnp.float32
        ).astype(jnp.bfloat16)
        inner_z = jnp.einsum(
            "wbc,wcd->wbd", chosen, right, preferred_element_type=jnp.float32
        ).astype(jnp.bfloat16)
        image = jnp.einsum("wab,wbd->ad", left_blocks, inner_z, preferred_element_type=jnp.float32)
        return image * live

    def evolve(left_blocks, start):
        first = start * live
        norm_start = lax.psum(inner(first, first), "sec") / count
        current = first / jnp.sqrt(norm_start + eps)
        previous = jnp.zeros_like(current)
        beta = jnp.float32(0.0)
        basis = [current]
        alphas = []
        betas = []
        for step in range(KRYLOV):
            image = apply_op(left_blocks, current)
            alpha = lax.psum(inner(current, image), "sec") / count
            squares = None
            alphas.append(alpha)
            if step + 1 < KRYLOV:
                remain = image - alpha * current - beta * previous
                squares = lax.psum(inner(remain, remain), "sec") / count
                beta = jnp.sqrt(squares + eps)
                betas.append(beta)
                previous = current
                current = remain / beta
                basis.append(current)
        coeffs = tridiag_coeffs(alphas, betas)
        mixed = coeffs[0] * basis[0]
        for index in range(1, KRYLOV):
            mixed = mixed + coeffs[index] * basis[index]
        return mixed / jnp.sqrt(jnp.sum(coeffs * coeffs))

    first = evolve(left, psi[0])
    first_bf = first.astype(jnp.bfloat16)
    carried = shifted(boundary_env(first_bf, right), "seg", 1)
    left_two = (left.astype(jnp.float32) + carried.astype(jnp.float32)).astype(jnp.bfloat16)
    second = evolve(left_two, first)
    return second[None]


def solution(mesh):
    in_specs = (
        P("seg", "sec", None),
        P("seg", None, "sec", None),
        P("seg", None, None, None),
        P(),
        P("seg", "sec"),
    )
    out_specs = P("seg", "sec", None)
    return jax.shard_map(
        per_device, mesh=mesh, in_specs=in_specs, out_specs=out_specs, check_vma=False
    )
```

profile of v0, /device:TPU:6, one launch (start us, length us, event | category | flops | bytes accessed | tf_op | source)
XLA Modules:
  0.0 1930.6 jit_solution(7260460981102785494)
XLA Ops:
  2.6 150.5 %psum.84 = f32[]{:T(128)} all-reduce(f32[]{:T(128)} %multiply_reduce_fusion.9), channel_id=1, replica_groups=mesh['seg'=8,'sec'=64] {'sec'}, use_global_device_ids=true, to_apply=%region_1.2 | all-reduce | flops 1 | bytes 8 | tf_op jit(solution)/shard_map/psum | solution.py:78
  161.5 4.5 collective-permute-done
  173.3 3.1 fusion.142
  176.4 5.7 multiply_reduce_fusion.8
  182.1 142.0 %psum.85 = f32[]{:T(128)} all-reduce(f32[]{:T(128)} %get-tuple-element.55), channel_id=1, replica_groups=mesh['seg'=8,'sec'=64] {'sec'}, use_global_device_ids=true, to_apply=%region_3.4 | all-reduce | flops 1 | bytes 8 | tf_op jit(solution)/shard_map/psum | solution.py:87
  326.4 138.5 %psum.86 = f32[]{:T(128)} all-reduce(f32[]{:T(128)} %multiply_reduce_fusion.7), channel_id=1, replica_groups=mesh['seg'=8,'sec'=64] {'sec'}, use_global_device_ids=true, to_apply=%region_5.6 | all-reduce | flops 1 | bytes 8 | tf_op jit(solution)/shard_map/psum | solution.py:92
  469.8 4.5 collective-permute-start.5
  474.4 5.4 collective-permute-start.7
  487.7 5.8 multiply_reduce_fusion.6
  493.5 154.4 %psum.87 = f32[]{:T(128)} all-reduce(f32[]{:T(128)} %get-tuple-element.57), channel_id=1, replica_groups=mesh['seg'=8,'sec'=64] {'sec'}, use_global_device_ids=true, to_apply=%region_7.8 | all-reduce | flops 1 | bytes 8 | tf_op jit(solution)/shard_map/psum | solution.py:87
  650.9 138.5 %psum.88 = f32[]{:T(128)} all-reduce(f32[]{:T(128)} %get-tuple-element.41), channel_id=1, replica_groups=mesh['seg'=8,'sec'=64] {'sec'}, use_global_device_ids=true, to_apply=%region_9.10 | all-reduce | flops 1 | bytes 8 | tf_op jit(solution)/shard_map/psum | solution.py:92
  792.8 3.9 collective-permute-start.9
  798.0 8.4 collective-permute-start.11
  814.9 5.1 fusion.115
  821.4 139.2 %psum.89 = f32[]{:T(128)} all-reduce(f32[]{:T(128)} %fusion.115), channel_id=1, replica_groups=mesh['seg'=8,'sec'=64] {'sec'}, use_global_device_ids=true, to_apply=%region_11.12 | all-reduce | flops 1 | bytes 8 | tf_op jit(solution)/shard_map/psum | solution.py:87
  967.3 4.2 multiply_reduce_fusion.4
  971.6 139.9 %psum.90 = f32[]{:T(128)} all-reduce(f32[]{:T(128)} %get-tuple-element.35), channel_id=1, replica_groups=mesh['seg'=8,'sec'=64] {'sec'}, use_global_device_ids=true, to_apply=%region_17.18 | all-reduce | flops 1 | bytes 8 | tf_op jit(solution)/shard_map/psum | solution.py:78
  1115.0 3.2 collective-permute-start.14
  1119.5 9.5 collective-permute-start.16
  1146.5 6.0 multiply_reduce_fusion.3
  1152.5 138.5 %psum.91 = f32[]{:T(128)} all-reduce(f32[]{:T(128)} %get-tuple-element.59), channel_id=1, replica_groups=mesh['seg'=8,'sec'=64] {'sec'}, use_global_device_ids=true, to_apply=%region_19.20 | all-reduce | flops 1 | bytes 8 | tf_op jit(solution)/shard_map/psum | solution.py:87
  1293.2 140.5 %psum.92 = f32[]{:T(128)} all-reduce(f32[]{:T(128)} %multiply_reduce_fusion.2), channel_id=1, replica_groups=mesh['seg'=8,'sec'=64] {'sec'}, use_global_device_ids=true, to_apply=%region_21.22 | all-reduce | flops 1 | bytes 8 | tf_op jit(solution)/shard_map/psum | solution.py:92
  1438.5 4.5 collective-permute-start.18
  1443.0 5.7 collective-permute-start.20
  1456.6 6.0 multiply_reduce_fusion.1
  1462.5 145.0 %psum.93 = f32[]{:T(128)} all-reduce(f32[]{:T(128)} %get-tuple-element.61), channel_id=1, replica_groups=mesh['seg'=8,'sec'=64] {'sec'}, use_global_device_ids=true, to_apply=%region_23.24 | all-reduce | flops 1 | bytes 8 | tf_op jit(solution)/shard_map/psum | solution.py:87
  1610.3 138.5 %psum.94 = f32[]{:T(128)} all-reduce(f32[]{:T(128)} %get-tuple-element.29), channel_id=1, replica_groups=mesh['seg'=8,'sec'=64] {'sec'}, use_global_device_ids=true, to_apply=%region_25.26 | all-reduce | flops 1 | bytes 8 | tf_op jit(solution)/shard_map/psum | solution.py:92
  1752.3 3.9 collective-permute-start.22
  1757.6 8.2 collective-permute-start.24
  1774.2 5.3 fusion.120
  1780.9 139.3 %psum.95 = f32[]{:T(128)} all-reduce(f32[]{:T(128)} %fusion.120), channel_id=1, replica_groups=mesh['seg'=8,'sec'=64] {'sec'}, use_global_device_ids=true, to_apply=%region_27.28 | all-reduce | flops 1 | bytes 8 | tf_op jit(solution)/shard_map/psum | solution.py:87
  1925.4 3.5 divide_bitcast_fusion
  (119 shorter events, 108.8 us)
Async XLA Ops:
  0.0 176.4 %copy-start = (bf16[1,26,256,256]{3,2,1,0:T(8,128)(2,1)S(1)}, bf16[1,26,256,256]{3,2,1,0:T(8,128)(2,1)}, u32[]{:S(2)}) copy-start(bf16[1,26,256,256]{3,2,1,0:T(8,128)(2,1)} %param.11) | copy-start | bytes 10223620
  0.0 173.3 %copy-start.2 = (s32[26]{0:T(128)S(1)}, s32[26]{0:T(128)}, u32[]{:S(2)}) copy-start(s32[26]{0:T(128)} %param.12) | copy-start | bytes 316
  154.5 15.2 collective-permute-start.3
  156.4 11.8 collective-permute-start.2
  157.7 9.8 collective-permute-start.1
  159.6 6.5 collective-permute-start
  467.2 12.6 collective-permute-start.4
  468.5 12.6 collective-permute-start.6
  469.8 10.7 collective-permute-start.5
  474.4 7.4 collective-permute-start.7
  791.5 16.8 collective-permute-start.10
  792.8 14.9 collective-permute-start.9
  796.7 10.4 collective-permute-start.8
  798.0 11.0 collective-permute-start.11
  1113.7 22.5 %collective-permute-start.15 = (bf16[128,256]{0,1:T(8,128)(2,1)}, bf16[128,256]{0,1:T(8,128)(2,1)}, u32[]{:S(2)}, u32[]{:S(2)}) collective-permute-start(bf16[128,256]{0,1:T(8,128)(2,1)} %get-tuple-element.34), channel_id=1, source_target_pairs={{8,0},{9,1},{10,2},{11,3},{12,4},{13,5},{14,6},{15,7},{16,8},{17,9... | collective-permute-start | bytes 196616 | tf_op jit(solution)/shard_map/ppermute | solution.py:18
  1115.0 20.6 %collective-permute-start.14 = (bf16[128,256]{0,1:T(8,128)(2,1)}, bf16[128,256]{0,1:T(8,128)(2,1)}, u32[]{:S(2)}, u32[]{:S(2)}) collective-permute-start(bf16[128,256]{0,1:T(8,128)(2,1)} %get-tuple-element.34), channel_id=1, source_target_pairs={{0,1},{1,2},{2,3},{3,4},{4,5},{5,6},{6,7},{7,8},{8,9},{9,10},{10,1... | collective-permute-start | bytes 196616 | tf_op jit(solution)/shard_map/ppermute | solution.py:18
  1118.2 15.9 collective-permute-start.13
  1119.5 18.2 collective-permute-start.16
  1132.1 14.5 copy-start.1
  1132.1 14.4 collective-permute-start.12
  1435.9 12.8 collective-permute-start.17
  1437.2 12.8 collective-permute-start.19
  1438.5 10.9 collective-permute-start.18
  1443.0 7.6 collective-permute-start.20
  1751.1 16.6 collective-permute-start.23
  1752.3 14.7 collective-permute-start.22
  1756.3 10.1 collective-permute-start.21
  1757.6 10.7 collective-permute-start.24
where the time goes:
time: 1930 us
  blocking collectives  1700 us (88%)
  starting transfers between devices  78.6 us (4%)
  matrix products  55.8 us (3%)
  other arithmetic  43.2 us (2%)
  local copies, waits for them, and re-layouts  31.3 us (2%)
    psum x6, blocking collectives, evolve(): alpha = lax.psum(inner(current, image), 'sec') / count  858 us
    psum x4, blocking collectives, evolve(): squares = lax.psum(inner(remain, remain), 'sec') / count  556 us
    psum x2, blocking collectives, evolve(): norm_start = lax.psum(inner(first, first), 'sec') / count  290 us
    ppermute x25, starting transfers between devices, shifted(): return lax.ppermute(shard, axis, pairs)  78.6 us
  transfers between devices with their start and end apart: 25, of which 2 were waited for; matrix products, arithmetic and copies ran while one was open for 1% of the time, Pallas kernels for 0%

commit v1 on v0

v1 whole, which is shorter than its diff:
```python
import functools

import jax
import jax.numpy as jnp
from jax import lax
from jax.experimental import pallas as pl
from jax.experimental.pallas import tpu as pltpu
from jax.sharding import PartitionSpec as P

MESH = pl.DeviceIdType.MESH

NDN = 8
KRYLOV = 3
EPS = 1e-06
SERIES_ORDER = 3
STEP_SIZE = 0.5
SHRINK = 2.0**-12
PAIRS = ((0, 0), (0, 1), (0, 2), (0, 3), (1, 1), (1, 2), (1, 3), (2, 2), (2, 3))


def quadratic(gram, first, second):
    total = None
    for i, a in enumerate(first):
        if a is None:
            continue
        inner = None
        for j, b in enumerate(second):
            if b is None:
                continue
            piece = b * gram[(min(i, j), max(i, j))]
            inner = piece if inner is None else inner + piece
        total = a * inner if total is None else total + a * inner
    return total


def coefficients(sums, count):
    norm = sums[(0, 0)] * (1.0 / count) + EPS
    over = 1.0 / norm
    gram = {pair: value * (1.0 / count) * over for pair, value in sums.items()}
    eps = EPS * SHRINK * SHRINK
    a0 = gram[(0, 1)]
    rest = gram[(1, 1)] - 2.0 * a0 * gram[(0, 1)] + a0 * a0 * gram[(0, 0)]
    b1 = jnp.sqrt(jnp.maximum(rest, 0.0) + eps)
    i1 = 1.0 / b1
    v1 = (-a0 * i1, i1)
    w1 = (None, -a0 * i1, i1)
    a1 = quadratic(gram, v1, w1)
    r1 = (-a1 * v1[0] - b1, w1[1] - a1 * v1[1], w1[2])
    rest = quadratic(gram, r1, r1)
    b2 = jnp.sqrt(jnp.maximum(rest, 0.0) + eps)
    i2 = 1.0 / b2
    v2 = tuple(x * i2 for x in r1)
    a2 = quadratic(gram, v2, (None,) + v2)
    a0, a1, a2, b1, b2 = (x * (1.0 / SHRINK) for x in (a0, a1, a2, b1, b2))
    term = (jnp.ones_like(a0), jnp.zeros_like(a0), jnp.zeros_like(a0))
    c = term
    for order in range(1, SERIES_ORDER + 1):
        factor = -STEP_SIZE / order
        term = (
            (a0 * term[0] + b1 * term[1]) * factor,
            (b1 * term[0] + a1 * term[1] + b2 * term[2]) * factor,
            (b2 * term[1] + a2 * term[2]) * factor,
        )
        c = tuple(x + y for x, y in zip(c, term))
    size = jnp.sqrt(c[0] * c[0] + c[1] * c[1] + c[2] * c[2])
    scale = 1.0 / (size * jnp.sqrt(norm))
    return (
        (c[0] + c[1] * v1[0] + c[2] * v2[0]) * scale,
        (c[1] * v1[1] + c[2] * v2[1]) * scale,
        c[2] * v2[2] * scale,
    )


def kernel(
    segs, sectors, kinds, rows, psi, left, right, out,
    r_v, l_v, z_v, src, chosen, u, env_out, env_in, red,
    load_sem, ex_send, ex_recv, red_send, red_recv, env_send, env_recv,
):
    width, blk, cols = l_v.shape[0], psi.shape[0], psi.shape[1]
    grid_rows = sectors // NDN
    seg, sec = lax.axis_index("seg"), lax.axis_index("sec")
    row, col = sec // NDN, sec % NDN
    count = 1.0 * sectors * blk * cols

    loads = [
        pltpu.make_async_copy(right, r_v, load_sem.at[0]),
        pltpu.make_async_copy(left, l_v, load_sem.at[1]),
    ]
    for load in loads:
        load.start()

    barrier = pltpu.get_barrier_semaphore()
    for j in range(1, NDN):
        other = row * NDN + lax.rem(col + j, NDN)
        pl.semaphore_signal(barrier, inc=1, device_id=(seg, other), device_id_type=MESH)
    for j in range(1, grid_rows):
        other = lax.rem(row + j, grid_rows) * NDN + col
        pl.semaphore_signal(barrier, inc=1, device_id=(seg, other), device_id_type=MESH)
    before = lax.rem(seg + segs - 1, segs)
    pl.semaphore_signal(barrier, inc=1, device_id=(before, sec), device_id_type=MESH)

    live = lax.broadcasted_iota(jnp.int32, (blk, cols), 0) < rows[0, 0]
    keep = jnp.where(live, SHRINK, 0.0)
    start = jnp.where(live, psi[...], 0.0)
    u[0] = start
    src[0, 0] = start.astype(jnp.bfloat16)

    neighbours = (
        (1, 1, col < NDN - 1),
        (2, -1, col > 0),
        (3, NDN, row < grid_rows - 1),
        (4, -NDN, row > 0),
    )
    for kind, _, there in neighbours:

        @pl.when(jnp.logical_not(there))
        def _():
            for step in (0, 1, 2, 4, 5):
                src[step, kind] = jnp.zeros((blk, cols), jnp.bfloat16)

    @pl.when(seg == 0)
    def _():
        env_in[...] = jnp.zeros(env_in.shape, env_in.dtype)

    pl.semaphore_wait(barrier, NDN - 1 + grid_rows - 1 + 1)

    def sending(step, kind, offset):
        return pltpu.make_async_remote_copy(
            src_ref=src.at[step, 0],
            dst_ref=src.at[step, kind],
            send_sem=ex_send.at[step, kind],
            recv_sem=ex_recv.at[step, kind],
            device_id=(seg, sec - offset),
            device_id_type=MESH,
        )

    mirrored = {1: col > 0, 2: col < NDN - 1, 3: row > 0, 4: row < grid_rows - 1}

    def exchange_start(step):
        for kind, offset, _ in (neighbours[2], neighbours[3], neighbours[0], neighbours[1]):

            @pl.when(mirrored[kind])
            def _():
                sending(step, kind, offset).start()

    def exchange_wait(step):
        for kind, offset, there in neighbours:

            @pl.when(there)
            def _():
                sending(step, kind, offset).wait_recv()

    def exchange_drain(step):
        for kind, offset, _ in neighbours:

            @pl.when(mirrored[kind])
            def _():
                sending(step, kind, offset).wait_send()

    def right_side(step):
        chosen[...] = src[step]
        for w in range(width):
            source = chosen[kinds[w]]
            z_v[w * blk : (w + 1) * blk, :] = jnp.dot(
                source, r_v[w], preferred_element_type=jnp.float32
            ).astype(jnp.bfloat16)

    def left_side():
        total = jnp.zeros((blk, cols), jnp.float32)
        for w in range(0, width, 2):
            pair = jnp.concatenate([l_v[w], l_v[w + 1]], axis=1)
            total = total + jnp.dot(
                pair, z_v[w * blk : (w + 2) * blk, :], preferred_element_type=jnp.float32
            )
        return total * keep

    def reduce(update):
        lanes = lax.broadcasted_iota(jnp.int32, (16, 128), 1)
        sublanes = lax.broadcasted_iota(jnp.int32, (16, 128), 0)
        parts = []
        for i, j in PAIRS:
            product = u[i] * u[j]
            product = product[:, :128] + product[:, 128:]
            parts.append(jnp.sum(product, axis=0, keepdims=True))
        parts.append(jnp.zeros((16 - len(PAIRS), 128), jnp.float32))
        table = jnp.concatenate(parts, axis=0)
        totals = jnp.sum(table, axis=1, keepdims=True)
        mine = jnp.sum(jnp.where(lanes == sublanes, totals, 0.0), axis=0, keepdims=True)
        for phase, (place, size) in enumerate(((col, NDN), (row, grid_rows))):
            buffer = red.at[update, phase]
            buffer[pl.ds(place, 1), :] = mine

            def passing(j, slot):
                other = lax.rem(place + j, size)
                other = row * NDN + other if phase == 0 else other * NDN + col
                return pltpu.make_async_remote_copy(
                    src_ref=buffer.at[pl.ds(place, 1), :],
                    dst_ref=buffer.at[pl.ds(slot, 1), :],
                    send_sem=red_send.at[update, phase, j],
                    recv_sem=red_recv.at[update, phase, j],
                    device_id=(seg, other),
                    device_id_type=MESH,
                )

            for j in range(1, size):
                passing(j, place).start()
            for j in range(1, size):
                passing(j, lax.rem(place - j + size, size)).wait_recv()
            for j in range(1, size):
                passing(j, place).wait_send()
            mine = jnp.sum(buffer[0:size, :], axis=0, keepdims=True)
        spread = jnp.where(lanes == sublanes, jnp.broadcast_to(mine, (16, 128)), 0.0)
        totals = jnp.broadcast_to(jnp.sum(spread, axis=1, keepdims=True), (16, 128))
        return {pair: totals[k : k + 1, :] for k, pair in enumerate(PAIRS)}

    def widen(coefficient):
        return jnp.concatenate([coefficient] * (cols // 128), axis=1)

    exchange_start(0)
    loads[0].wait()
    loads[1].wait()

    def first_step(step, carry):
        exchange_wait(step)
        right_side(step)
        image = left_side()
        u[step + 1] = image

        @pl.when(step < KRYLOV - 1)
        def _():
            src[step + 1, 0] = image.astype(jnp.bfloat16)
            exchange_start(step + 1)

        return carry

    lax.fori_loop(0, KRYLOV, first_step, 0)
    mix = [widen(x) for x in coefficients(reduce(0), count)]
    first = mix[0] * u[0] + mix[1] * u[1] + mix[2] * u[2]
    first_bf = first.astype(jnp.bfloat16)

    scale = (cols * blk * width) ** (-0.5)
    half = width // 2

    def passing_env(part):
        piece = pl.ds(part * half, half)
        return pltpu.make_async_remote_copy(
            src_ref=env_out.at[piece],
            dst_ref=env_in.at[piece],
            send_sem=env_send.at[part],
            recv_sem=env_recv.at[part],
            device_id=(lax.rem(seg + 1, segs), sec),
            device_id_type=MESH,
        )

    for part in range(2):
        for w in range(part * half, (part + 1) * half):
            projected = jnp.dot(first_bf, r_v[w], preferred_element_type=jnp.float32).astype(jnp.bfloat16)
            env = lax.dot_general(
                projected, first_bf, (((1,), (1,)), ((), ())), preferred_element_type=jnp.float32
            )
            env_out[w] = (env * scale).astype(jnp.bfloat16)

        @pl.when(seg < segs - 1)
        def _():
            passing_env(part).start()

    for kind in range(1, 5):
        mixed = mix[0] * src[0, kind].astype(jnp.float32)
        mixed = mixed + mix[1] * src[1, kind].astype(jnp.float32)
        mixed = mixed + mix[2] * src[2, kind].astype(jnp.float32)
        src[3, kind] = mixed.astype(jnp.bfloat16)
    src[3, 0] = first_bf
    u[0] = first
    right_side(3)

    @pl.when(seg > 0)
    def _():
        passing_env(0).wait_recv()
        passing_env(1).wait_recv()

    for w in range(width):
        l_v[w] = (l_v[w].astype(jnp.float32) + env_in[w].astype(jnp.float32)).astype(jnp.bfloat16)
    image = left_side()
    u[1] = image
    src[4, 0] = image.astype(jnp.bfloat16)
    exchange_start(4)

    def second_step(step, carry):
        exchange_wait(step)
        right_side(step)
        image = left_side()
        u[step - 2] = image

        @pl.when(step < 5)
        def _():
            src[step + 1, 0] = image.astype(jnp.bfloat16)
            exchange_start(step + 1)

        return carry

    lax.fori_loop(4, 6, second_step, 0)
    mix = [widen(x) for x in coefficients(reduce(1), count)]
    out[...] = mix[0] * u[0] + mix[1] * u[1] + mix[2] * u[2]

    for step in (0, 1, 2, 4, 5):
        exchange_drain(step)

    @pl.when(seg < segs - 1)
    def _():
        passing_env(0).wait_send()
        passing_env(1).wait_send()


def per_device(segs, sectors, psi, left_env, right_env, term_kind, block_rows):
    _, blk, cols = psi.shape
    width = left_env.shape[1]
    grid_rows = sectors // NDN
    vmem = pl.BlockSpec(memory_space=pltpu.VMEM)
    smem = pl.BlockSpec(memory_space=pltpu.SMEM)
    anywhere = pl.BlockSpec(memory_space=pl.ANY)
    result = pl.pallas_call(
        functools.partial(kernel, segs, sectors),
        out_shape=jax.ShapeDtypeStruct((blk, cols), jnp.float32),
        in_specs=[smem, smem, vmem, anywhere, anywhere],
        out_specs=vmem,
        scratch_shapes=[
            pltpu.VMEM((width, cols, cols), jnp.bfloat16),
            pltpu.VMEM((width, blk, blk), jnp.bfloat16),
            pltpu.VMEM((width * blk, cols), jnp.bfloat16),
            pltpu.VMEM((6, 5, blk, cols), jnp.bfloat16),
            pltpu.VMEM((5, blk, cols), jnp.bfloat16),
            pltpu.VMEM((KRYLOV + 1, blk, cols), jnp.float32),
            pltpu.VMEM((width, blk, blk), jnp.bfloat16),
            pltpu.VMEM((width, blk, blk), jnp.bfloat16),
            pltpu.VMEM((2, 2, 8, 128), jnp.float32),
            pltpu.SemaphoreType.DMA((2,)),
            pltpu.SemaphoreType.DMA((6, 5)),
            pltpu.SemaphoreType.DMA((6, 5)),
            pltpu.SemaphoreType.DMA((2, 2, max(NDN, grid_rows))),
            pltpu.SemaphoreType.DMA((2, 2, max(NDN, grid_rows))),
            pltpu.SemaphoreType.DMA((2,)),
            pltpu.SemaphoreType.DMA((2,)),
        ],
        compiler_params=pltpu.CompilerParams(
            collective_id=0, has_side_effects=True, vmem_limit_bytes=48 * 2**20
        ),
    )(term_kind, block_rows, psi[0], left_env[0], right_env[0])
    return result[None]


def solution(mesh):
    in_specs = (
        P("seg", "sec", None),
        P("seg", None, "sec", None),
        P("seg", None, None, None),
        P(),
        P("seg", "sec"),
    )
    out_specs = P("seg", "sec", None)
    return jax.shard_map(
        functools.partial(per_device, mesh.shape["seg"], mesh.shape["sec"]),
        mesh=mesh, in_specs=in_specs, out_specs=out_specs, check_vma=False,
    )
```

time: 1930 us -> 88.4 us (0.05)
  blocking collectives: 1700 us -> 0 us
  Pallas kernels: 0 us -> 82.2 us
  starting transfers between devices: 78.6 us -> 0 us
  matrix products: 55.8 us -> 0 us
  other arithmetic: 43.2 us -> 0 us
  local copies, waits for them, and re-layouts: 31.3 us -> 5.33 us
    psum x12 -> x0, blocking collectives: 1700 us -> none  [the longest x6 858 us: evolve(): alpha = lax.psum(inner(current, image), 'sec') / count]
    pallas_call x0 -> x1, Pallas kernels: none -> 82.2 us  [per_device(): pl.pallas_call(functools.partial(kernel, segs, sectors), out_shape=jax.Sh...]
    ppermute x25 -> x0, starting transfers between devices: 78.6 us -> none  [shifted(): return lax.ppermute(shard, axis, pairs)]
    dot_general x13 -> x0, matrix products: 55.8 us -> none  [the longest x6 34 us: apply_op(): jnp.einsum('wab,wbd->ad', left_blocks, inner_z, preferred_element_type=jn...]
    reduce_sum x14 -> x0, other arithmetic: 19.8 us -> none  [the longest x6 12.7 us: inner(): return jnp.sum(first * second)]
  transfers between devices with their start and end apart: 25 -> 0, of which waited for: 2 -> 0; matrix products, arithmetic and copies ran while one was open for 1% -> 0% of each run, Pallas kernels for 0% -> 0%
where the time goes in v1:
time: 88.4 us; the launch traced here: 88.2 us
  Pallas kernels  82.2 us (93%)
  local copies, waits for them, and re-layouts  5.33 us (6%)
    pallas_call x1, Pallas kernels, per_device(): pl.pallas_call(functools.partial(kernel, segs, sectors), out_shape=jax.Sh...  82.2 us
    unnamed x9, local copies, waits for them, and re-layouts  5.33 us

profile of v1, /device:TPU:6, one launch (start us, length us, event | category | flops | bytes accessed | tf_op | source)
XLA Modules:
  0.0 88.2 jit_solution(3374421085885572751)
XLA Ops:
  0.7 0.0 copy-start
  0.7 2.0 %copy-done = bf16[1,26,256,256]{3,2,1,0:T(8,128)(2,1)S(1)} copy-done((bf16[1,26,256,256]{3,2,1,0:T(8,128)(2,1)S(1)}, bf16[1,26,256,256]{3,2,1,0:T(8,128)(2,1)}, u32[]{:S(2)}) %copy-start) | copy-done | bytes 3407896
  2.6 0.0 copy-start.1
  2.6 1.2 %copy-done.1 = bf16[1,26,128,128]{3,2,1,0:T(8,128)(2,1)S(1)} copy-done((bf16[1,26,128,128]{3,2,1,0:T(8,128)(2,1)S(1)}, bf16[1,26,128,128]{3,2,1,0:T(8,128)(2,1)}, u32[]{:S(2)}) %copy-start.1) | copy-done | bytes 851992
  3.8 0.0 copy-start.2
  3.8 0.9 %copy-done.2 = f32[1,128,256]{2,1,0:T(8,128)S(1)} copy-done((f32[1,128,256]{2,1,0:T(8,128)S(1)}, f32[1,128,256]{2,1,0:T(8,128)}, u32[]{:S(2)}) %copy-start.2) | copy-done | bytes 131096
  4.7 0.0 copy-start.3
  4.7 0.7 copy-done.3
  5.3 82.2 %shard_map.55 = f32[128,256]{1,0:T(8,128)S(1)} custom-call(s32[26]{0:T(128)S(1)} %copy-done.3, s32[1,1]{1,0:T(1,128)S(6)} %copy.7.rows, f32[128,256]{1,0:T(8,128)S(1)} %bitcast.7, bf16[26,128,128]{2,1,0:T(8,128)(2,1)S(1)} %bitcast.5, bf16[26,256,256]{2,1,0:T(8,128)(2,1)S(1)} %bitcast.4), custom_call_target="tpu_custom_call" | custom-call | tf_op jit(solution)/shard_map/pallas_call | solution.py:321
  87.5 0.7 copy.8
Async XLA Ops:
  0.7 2.0 %copy-start = (bf16[1,26,256,256]{3,2,1,0:T(8,128)(2,1)S(1)}, bf16[1,26,256,256]{3,2,1,0:T(8,128)(2,1)}, u32[]{:S(2)}) copy-start(bf16[1,26,256,256]{3,2,1,0:T(8,128)(2,1)} %param.7) | copy-start | bytes 10223620
  2.6 1.2 %copy-start.1 = (bf16[1,26,128,128]{3,2,1,0:T(8,128)(2,1)S(1)}, bf16[1,26,128,128]{3,2,1,0:T(8,128)(2,1)}, u32[]{:S(2)}) copy-start(bf16[1,26,128,128]{3,2,1,0:T(8,128)(2,1)} %param.6) | copy-start | bytes 2555908
  3.8 0.9 %copy-start.2 = (f32[1,128,256]{2,1,0:T(8,128)S(1)}, f32[1,128,256]{2,1,0:T(8,128)}, u32[]{:S(2)}) copy-start(f32[1,128,256]{2,1,0:T(8,128)} %param.5) | copy-start | bytes 393220
  4.7 0.7 copy-start.3

commit v2 on v1

--- a/solution.py
+++ b/solution.py
@@ -14,6 +14,7 @@
 EPS = 1e-06
 SERIES_ORDER = 3
 STEP_SIZE = 0.5
+VMEM_LIMIT = 63 * 2**20
 SHRINK = 2.0**-12
 PAIRS = ((0, 0), (0, 1), (0, 2), (0, 3), (1, 1), (1, 2), (1, 3), (2, 2), (2, 3))
 
@@ -72,57 +73,55 @@
 
 
 def kernel(
-    segs, sectors, kinds, rows, psi, left, right, out,
-    r_v, l_v, z_v, src, chosen, u, env_out, env_in, red,
-    load_sem, ex_send, ex_recv, red_send, red_recv, env_send, env_recv,
+    segs, sectors, kinds_in, rows_in, psi, left, right, out,
+    kinds, rows, start_v, r_v, l_v, z_v, src, chosen, u, env_out, env_in, table, red,
+    load_sem, ex_send, ex_recv, red_send, red_recv, env_send, env_recv, hello,
 ):
-    width, blk, cols = l_v.shape[0], psi.shape[0], psi.shape[1]
+    width, blk, cols = l_v.shape[0], l_v.shape[1], r_v.shape[2]
     grid_rows = sectors // NDN
     seg, sec = lax.axis_index("seg"), lax.axis_index("sec")
     row, col = sec // NDN, sec % NDN
     count = 1.0 * sectors * blk * cols
 
+    def beside(rows_on):
+        return (seg, lax.rem(row + rows_on + grid_rows, grid_rows) * NDN + col)
+
     loads = [
-        pltpu.make_async_copy(right, r_v, load_sem.at[0]),
-        pltpu.make_async_copy(left, l_v, load_sem.at[1]),
+        pltpu.make_async_copy(psi, start_v, load_sem.at[0]),
+        pltpu.make_async_copy(rows_in, rows, load_sem.at[1]),
+        pltpu.make_async_copy(kinds_in, kinds, load_sem.at[2]),
+        pltpu.make_async_copy(right, r_v, load_sem.at[3]),
+        pltpu.make_async_copy(left, l_v, load_sem.at[4]),
     ]
-    for load in loads:
-        load.start()
+    loads[0].start()
+    loads[1].start()
 
     barrier = pltpu.get_barrier_semaphore()
+    for rows_on in (-1, 1):
+        pl.semaphore_signal(barrier, inc=1, device_id=beside(rows_on), device_id_type=MESH)
     for j in range(1, NDN):
         other = row * NDN + lax.rem(col + j, NDN)
         pl.semaphore_signal(barrier, inc=1, device_id=(seg, other), device_id_type=MESH)
-    for j in range(1, grid_rows):
-        other = lax.rem(row + j, grid_rows) * NDN + col
-        pl.semaphore_signal(barrier, inc=1, device_id=(seg, other), device_id_type=MESH)
     before = lax.rem(seg + segs - 1, segs)
     pl.semaphore_signal(barrier, inc=1, device_id=(before, sec), device_id_type=MESH)
 
+    for load in loads[2:]:
+        load.start()
+    loads[0].wait()
+    loads[1].wait()
     live = lax.broadcasted_iota(jnp.int32, (blk, cols), 0) < rows[0, 0]
-    keep = jnp.where(live, SHRINK, 0.0)
-    start = jnp.where(live, psi[...], 0.0)
-    u[0] = start
+    start = jnp.where(live, start_v[...], 0.0)
     src[0, 0] = start.astype(jnp.bfloat16)
 
+    pl.semaphore_wait(barrier, 2 + NDN - 1 + 1)
+
     neighbours = (
+        (3, NDN, row < grid_rows - 1),
+        (4, -NDN, row > 0),
         (1, 1, col < NDN - 1),
         (2, -1, col > 0),
-        (3, NDN, row < grid_rows - 1),
-        (4, -NDN, row > 0),
     )
-    for kind, _, there in neighbours:
-
-        @pl.when(jnp.logical_not(there))
-        def _():
-            for step in (0, 1, 2, 4, 5):
-                src[step, kind] = jnp.zeros((blk, cols), jnp.bfloat16)
-
-    @pl.when(seg == 0)
-    def _():
-        env_in[...] = jnp.zeros(env_in.shape, env_in.dtype)
-
-    pl.semaphore_wait(barrier, NDN - 1 + grid_rows - 1 + 1)
+    mirrored = {1: col > 0, 2: col < NDN - 1, 3: row > 0, 4: row < grid_rows - 1}
 
     def sending(step, kind, offset):
         return pltpu.make_async_remote_copy(
@@ -134,10 +133,8 @@
             device_id_type=MESH,
         )
 
-    mirrored = {1: col > 0, 2: col < NDN - 1, 3: row > 0, 4: row < grid_rows - 1}
-
     def exchange_start(step):
-        for kind, offset, _ in (neighbours[2], neighbours[3], neighbours[0], neighbours[1]):
+        for kind, offset, _ in neighbours:
 
             @pl.when(mirrored[kind])
             def _():
@@ -156,6 +153,15 @@
             @pl.when(mirrored[kind])
             def _():
                 sending(step, kind, offset).wait_send()
+
+    strides = (1, 2, 1)
+
+    def hello_start(turn):
+        for rows_on in (-strides[turn], strides[turn]):
+            pl.semaphore_signal(hello.at[turn], inc=1, device_id=beside(rows_on), device_id_type=MESH)
+
+    def hello_wait(turn):
+        pl.semaphore_wait(hello.at[turn], 2)
 
     def right_side(step):
         chosen[...] = src[step]
@@ -172,44 +178,48 @@
             total = total + jnp.dot(
                 pair, z_v[w * blk : (w + 2) * blk, :], preferred_element_type=jnp.float32
             )
-        return total * keep
+        keep = lax.broadcasted_iota(jnp.int32, (blk, cols), 0) < rows[0, 0]
+        return total * jnp.where(keep, SHRINK, 0.0)
+
+    def products(last):
+        for k, (i, j) in enumerate(PAIRS):
+            if j == last:
+                product = u[i] * u[j]
+                product = product[:, :128] + product[:, 128:]
+                table[k : k + 1, :] = jnp.sum(product, axis=0, keepdims=True)
+
+    lanes = lax.broadcasted_iota(jnp.int32, (16, 128), 1)
+    sublanes = lax.broadcasted_iota(jnp.int32, (16, 128), 0)
 
     def reduce(update):
-        lanes = lax.broadcasted_iota(jnp.int32, (16, 128), 1)
-        sublanes = lax.broadcasted_iota(jnp.int32, (16, 128), 0)
-        parts = []
-        for i, j in PAIRS:
-            product = u[i] * u[j]
-            product = product[:, :128] + product[:, 128:]
-            parts.append(jnp.sum(product, axis=0, keepdims=True))
-        parts.append(jnp.zeros((16 - len(PAIRS), 128), jnp.float32))
-        table = jnp.concatenate(parts, axis=0)
-        totals = jnp.sum(table, axis=1, keepdims=True)
+        buffer = red.at[update]
+        totals = jnp.sum(table[...], axis=1, keepdims=True)
         mine = jnp.sum(jnp.where(lanes == sublanes, totals, 0.0), axis=0, keepdims=True)
-        for phase, (place, size) in enumerate(((col, NDN), (row, grid_rows))):
-            buffer = red.at[update, phase]
-            buffer[pl.ds(place, 1), :] = mine
-
-            def passing(j, slot):
-                other = lax.rem(place + j, size)
-                other = row * NDN + other if phase == 0 else other * NDN + col
-                return pltpu.make_async_remote_copy(
-                    src_ref=buffer.at[pl.ds(place, 1), :],
-                    dst_ref=buffer.at[pl.ds(slot, 1), :],
-                    send_sem=red_send.at[update, phase, j],
-                    recv_sem=red_recv.at[update, phase, j],
-                    device_id=(seg, other),
-                    device_id_type=MESH,
-                )
-
-            for j in range(1, size):
-                passing(j, place).start()
-            for j in range(1, size):
-                passing(j, lax.rem(place - j + size, size)).wait_recv()
-            for j in range(1, size):
-                passing(j, place).wait_send()
-            mine = jnp.sum(buffer[0:size, :], axis=0, keepdims=True)
-        spread = jnp.where(lanes == sublanes, jnp.broadcast_to(mine, (16, 128)), 0.0)
+        buffer[pl.ds(sec, 1), :] = mine
+
+        def pass_on(turn, carry):
+            far = (turn + 1) // 2
+            offset = sectors // 2 + far - 2 * far * lax.rem(turn, 2)
+            pltpu.make_async_remote_copy(
+                src_ref=buffer.at[pl.ds(sec, 1), :],
+                dst_ref=buffer.at[pl.ds(sec, 1), :],
+                send_sem=red_send.at[update],
+                recv_sem=red_recv.at[update],
+                device_id=(seg, lax.rem(sec + offset, sectors)),
+                device_id_type=MESH,
+            ).start()
+            return carry
+
+        lax.fori_loop(0, sectors - 1, pass_on, 0)
+        others = buffer.at[pl.ds(0, sectors - 1), :]
+        every = pltpu.make_async_remote_copy(
+            src_ref=others, dst_ref=others, send_sem=red_send.at[update], recv_sem=red_recv.at[update],
+            device_id=(seg, lax.rem(sec + 1, sectors)), device_id_type=MESH,
+        )
+        every.wait_recv()
+        every.wait_send()
+        total = jnp.sum(buffer[...], axis=0, keepdims=True)
+        spread = jnp.where(lanes == sublanes, jnp.broadcast_to(total, (16, 128)), 0.0)
         totals = jnp.broadcast_to(jnp.sum(spread, axis=1, keepdims=True), (16, 128))
         return {pair: totals[k : k + 1, :] for k, pair in enumerate(PAIRS)}
 
@@ -217,23 +227,37 @@
         return jnp.concatenate([coefficient] * (cols // 128), axis=1)
 
     exchange_start(0)
-    loads[0].wait()
-    loads[1].wait()
-
-    def first_step(step, carry):
+    hello_start(0)
+    u[0] = start
+    table[...] = jnp.zeros(table.shape, table.dtype)
+    products(0)
+    for kind, _, there in neighbours:
+
+        @pl.when(jnp.logical_not(there))
+        def _():
+            for step in (0, 1, 2, 4, 5):
+                src[step, kind] = jnp.zeros((blk, cols), jnp.bfloat16)
+
+    @pl.when(seg == 0)
+    def _():
+        env_in[...] = jnp.zeros(env_in.shape, env_in.dtype)
+
+    for load in loads[2:]:
+        load.wait()
+
+    for step in range(KRYLOV):
         exchange_wait(step)
+        hello_wait(step)
+        if step + 1 < KRYLOV:
+            hello_start(step + 1)
         right_side(step)
         image = left_side()
-        u[step + 1] = image
-
-        @pl.when(step < KRYLOV - 1)
-        def _():
+        if step + 1 < KRYLOV:
             src[step + 1, 0] = image.astype(jnp.bfloat16)
             exchange_start(step + 1)
-
-        return carry
-
-    lax.fori_loop(0, KRYLOV, first_step, 0)
+        u[step + 1] = image
+        products(step + 1)
+
     mix = [widen(x) for x in coefficients(reduce(0), count)]
     first = mix[0] * u[0] + mix[1] * u[1] + mix[2] * u[2]
     first_bf = first.astype(jnp.bfloat16)
@@ -272,6 +296,7 @@
     src[3, 0] = first_bf
     u[0] = first
     right_side(3)
+    products(0)
 
     @pl.when(seg > 0)
     def _():
@@ -280,25 +305,18 @@
 
     for w in range(width):
         l_v[w] = (l_v[w].astype(jnp.float32) + env_in[w].astype(jnp.float32)).astype(jnp.bfloat16)
-    image = left_side()
-    u[1] = image
-    src[4, 0] = image.astype(jnp.bfloat16)
-    exchange_start(4)
-
-    def second_step(step, carry):
-        exchange_wait(step)
-        right_side(step)
+
+    for step in range(KRYLOV):
+        if step > 0:
+            exchange_wait(step + 3)
+            right_side(step + 3)
         image = left_side()
-        u[step - 2] = image
-
-        @pl.when(step < 5)
-        def _():
-            src[step + 1, 0] = image.astype(jnp.bfloat16)
-            exchange_start(step + 1)
-
-        return carry
-
-    lax.fori_loop(4, 6, second_step, 0)
+        if step + 1 < KRYLOV:
+            src[step + 4, 0] = image.astype(jnp.bfloat16)
+            exchange_start(step + 4)
+        u[step + 1] = image
+        products(step + 1)
+
     mix = [widen(x) for x in coefficients(reduce(1), count)]
     out[...] = mix[0] * u[0] + mix[1] * u[1] + mix[2] * u[2]
 
@@ -314,16 +332,16 @@
 def per_device(segs, sectors, psi, left_env, right_env, term_kind, block_rows):
     _, blk, cols = psi.shape
     width = left_env.shape[1]
-    grid_rows = sectors // NDN
-    vmem = pl.BlockSpec(memory_space=pltpu.VMEM)
-    smem = pl.BlockSpec(memory_space=pltpu.SMEM)
     anywhere = pl.BlockSpec(memory_space=pl.ANY)
     result = pl.pallas_call(
         functools.partial(kernel, segs, sectors),
         out_shape=jax.ShapeDtypeStruct((blk, cols), jnp.float32),
-        in_specs=[smem, smem, vmem, anywhere, anywhere],
-        out_specs=vmem,
+        in_specs=[anywhere] * 5,
+        out_specs=pl.BlockSpec(memory_space=pltpu.VMEM),
         scratch_shapes=[
+            pltpu.SMEM((width,), jnp.int32),
+            pltpu.SMEM((1, 1), jnp.int32),
+            pltpu.VMEM((blk, cols), jnp.float32),
             pltpu.VMEM((width, cols, cols), jnp.bfloat16),
             pltpu.VMEM((width, blk, blk), jnp.bfloat16),
             pltpu.VMEM((width * blk, cols), jnp.bfloat16),
@@ -332,17 +350,19 @@
             pltpu.VMEM((KRYLOV + 1, blk, cols), jnp.float32),
             pltpu.VMEM((width, blk, blk), jnp.bfloat16),
             pltpu.VMEM((width, blk, blk), jnp.bfloat16),
-            pltpu.VMEM((2, 2, 8, 128), jnp.float32),
-            pltpu.SemaphoreType.DMA((2,)),
+            pltpu.VMEM((16, 128), jnp.float32),
+            pltpu.VMEM((2, sectors, 128), jnp.float32),
+            pltpu.SemaphoreType.DMA((5,)),
             pltpu.SemaphoreType.DMA((6, 5)),
             pltpu.SemaphoreType.DMA((6, 5)),
-            pltpu.SemaphoreType.DMA((2, 2, max(NDN, grid_rows))),
-            pltpu.SemaphoreType.DMA((2, 2, max(NDN, grid_rows))),
             pltpu.SemaphoreType.DMA((2,)),
             pltpu.SemaphoreType.DMA((2,)),
+            pltpu.SemaphoreType.DMA((2,)),
+            pltpu.SemaphoreType.DMA((2,)),
+            pltpu.SemaphoreType.REGULAR((3,)),
         ],
         compiler_params=pltpu.CompilerParams(
-            collective_id=0, has_side_effects=True, vmem_limit_bytes=48 * 2**20
+            collective_id=0, has_side_effects=True, vmem_limit_bytes=VMEM_LIMIT
         ),
     )(term_kind, block_rows, psi[0], left_env[0], right_env[0])
     return result[None]

time: 88.4 us -> 79 us (0.89)
  Pallas kernels: 82.2 us -> 76 us
  local copies, waits for them, and re-layouts: 5.33 us -> 1.57 us
    pallas_call x1, Pallas kernels: 82.2 us -> 76 us  [per_device(): pl.pallas_call(functools.partial(kernel, segs, sectors), out_shape=jax.Sh...]
    unnamed x9 -> x1, local copies, waits for them, and re-layouts: 5.33 us -> 1.57 us
where the time goes in v2:
time: 79 us; the launch traced here: 78.2 us
  Pallas kernels  76 us (96%)
  local copies, waits for them, and re-layouts  1.57 us (2%)
    pallas_call x1, Pallas kernels, per_device(): pl.pallas_call(functools.partial(kernel, segs, sectors), out_shape=jax.Sh...  76 us

profile of v2, /device:TPU:6, one launch (start us, length us, event | category | flops | bytes accessed | tf_op | source)
XLA Modules:
  0.0 78.2 jit_solution(7218113529734932355)
XLA Ops:
  0.7 76.0 %shard_map.55 = f32[128,256]{1,0:T(8,128)} custom-call(s32[26]{0:T(128)} %kinds_in.1, s32[1,1]{1,0:T(1,128)S(6)} %copy.7.rows_in, f32[128,256]{1,0:T(8,128)} %bitcast.7, bf16[26,128,128]{2,1,0:T(8,128)(2,1)} %bitcast.5, bf16[26,256,256]{2,1,0:T(8,128)(2,1)} %bitcast.4), custom_call_target="tpu_custom_call" | custom-call | tf_op jit(solution)/shard_map/pallas_call | solution.py:336
  76.6 1.6 %copy.8 = f32[1,128,256]{2,1,0:T(8,128)} copy(f32[1,128,256]{2,1,0:T(8,128)} %bitcast.6) | data formatting | bytes 262144

commit v3 on v2

--- a/solution.py
+++ b/solution.py
@@ -16,6 +16,8 @@
 STEP_SIZE = 0.5
 VMEM_LIMIT = 63 * 2**20
 SHRINK = 2.0**-12
+AHEAD = 20
+AHEAD_PARTS = 4
 PAIRS = ((0, 0), (0, 1), (0, 2), (0, 3), (1, 1), (1, 2), (1, 3), (2, 2), (2, 3))
 
 
@@ -74,8 +76,8 @@
 
 def kernel(
     segs, sectors, kinds_in, rows_in, psi, left, right, out,
-    kinds, rows, start_v, r_v, l_v, z_v, src, chosen, u, env_out, env_in, table, red,
-    load_sem, ex_send, ex_recv, red_send, red_recv, env_send, env_recv, hello,
+    kinds, rows, start_v, r_v, l_v, z_v, src, chosen, u, r_prev, first_prev, env_out, env_in, table, red,
+    load_sem, ex_send, ex_recv, red_send, red_recv, ahead_send, ahead_recv, env_send, env_recv, hello,
 ):
     width, blk, cols = l_v.shape[0], l_v.shape[1], r_v.shape[2]
     grid_rows = sectors // NDN
@@ -226,7 +228,42 @@
     def widen(coefficient):
         return jnp.concatenate([coefficient] * (cols // 128), axis=1)
 
+    following = (lax.rem(seg + 1, segs), sec)
+    ahead = min(AHEAD, width - 2)
+    bounds = [ahead * part // AHEAD_PARTS for part in range(AHEAD_PARTS + 1)]
+
+    def passing_right(part):
+        piece = pl.ds(bounds[part], bounds[part + 1] - bounds[part])
+        return pltpu.make_async_remote_copy(
+            src_ref=right.at[piece], dst_ref=r_prev.at[piece],
+            send_sem=ahead_send.at[part], recv_sem=ahead_recv.at[part],
+            device_id=following, device_id_type=MESH,
+        )
+
+    def passing_first():
+        return pltpu.make_async_remote_copy(
+            src_ref=src.at[3, 0], dst_ref=first_prev, send_sem=env_send.at[0], recv_sem=env_recv.at[0],
+            device_id=following, device_id_type=MESH,
+        )
+
+    def passing_env():
+        return pltpu.make_async_remote_copy(
+            src_ref=env_out, dst_ref=env_in, send_sem=env_send.at[1], recv_sem=env_recv.at[1],
+            device_id=following, device_id_type=MESH,
+        )
+
+    def boundary(vector, block):
+        projected = jnp.dot(vector, block, preferred_element_type=jnp.float32).astype(jnp.bfloat16)
+        env = lax.dot_general(projected, vector, (((1,), (1,)), ((), ())), preferred_element_type=jnp.float32)
+        return (env * (cols * blk * width) ** (-0.5)).astype(jnp.bfloat16)
+
     exchange_start(0)
+
+    @pl.when(seg < segs - 1)
+    def _():
+        for part in range(AHEAD_PARTS):
+            passing_right(part).start()
+
     hello_start(0)
     u[0] = start
     table[...] = jnp.zeros(table.shape, table.dtype)
@@ -237,10 +274,6 @@
         def _():
             for step in (0, 1, 2, 4, 5):
                 src[step, kind] = jnp.zeros((blk, cols), jnp.bfloat16)
-
-    @pl.when(seg == 0)
-    def _():
-        env_in[...] = jnp.zeros(env_in.shape, env_in.dtype)
 
     for load in loads[2:]:
         load.wait()
@@ -262,49 +295,37 @@
     first = mix[0] * u[0] + mix[1] * u[1] + mix[2] * u[2]
     first_bf = first.astype(jnp.bfloat16)
 
-    scale = (cols * blk * width) ** (-0.5)
-    half = width // 2
-
-    def passing_env(part):
-        piece = pl.ds(part * half, half)
-        return pltpu.make_async_remote_copy(
-            src_ref=env_out.at[piece],
-            dst_ref=env_in.at[piece],
-            send_sem=env_send.at[part],
-            recv_sem=env_recv.at[part],
-            device_id=(lax.rem(seg + 1, segs), sec),
-            device_id_type=MESH,
-        )
-
-    for part in range(2):
-        for w in range(part * half, (part + 1) * half):
-            projected = jnp.dot(first_bf, r_v[w], preferred_element_type=jnp.float32).astype(jnp.bfloat16)
-            env = lax.dot_general(
-                projected, first_bf, (((1,), (1,)), ((), ())), preferred_element_type=jnp.float32
-            )
-            env_out[w] = (env * scale).astype(jnp.bfloat16)
-
-        @pl.when(seg < segs - 1)
-        def _():
-            passing_env(part).start()
+    src[3, 0] = first_bf
+
+    @pl.when(seg < segs - 1)
+    def _():
+        passing_first().start()
+        for w in range(ahead, width):
+            env_out[w - ahead] = boundary(first_bf, r_v[w])
+        passing_env().start()
 
     for kind in range(1, 5):
         mixed = mix[0] * src[0, kind].astype(jnp.float32)
         mixed = mixed + mix[1] * src[1, kind].astype(jnp.float32)
         mixed = mixed + mix[2] * src[2, kind].astype(jnp.float32)
         src[3, kind] = mixed.astype(jnp.bfloat16)
-    src[3, 0] = first_bf
     u[0] = first
     right_side(3)
     products(0)
 
     @pl.when(seg > 0)
     def _():
-        passing_env(0).wait_recv()
-        passing_env(1).wait_recv()
-
-    for w in range(width):
-        l_v[w] = (l_v[w].astype(jnp.float32) + env_in[w].astype(jnp.float32)).astype(jnp.bfloat16)
+        for part in range(AHEAD_PARTS):
+            passing_right(part).wait_recv()
+        passing_first().wait_recv()
+        vector = first_prev[...]
+        for w in range(ahead):
+            env = boundary(vector, r_prev[w])
+            l_v[w] = (l_v[w].astype(jnp.float32) + env.astype(jnp.float32)).astype(jnp.bfloat16)
+        passing_env().wait_recv()
+        for w in range(ahead, width):
+            env = env_in[w - ahead]
+            l_v[w] = (l_v[w].astype(jnp.float32) + env.astype(jnp.float32)).astype(jnp.bfloat16)
 
     for step in range(KRYLOV):
         if step > 0:
@@ -325,13 +346,16 @@
 
     @pl.when(seg < segs - 1)
     def _():
-        passing_env(0).wait_send()
-        passing_env(1).wait_send()
+        for part in range(AHEAD_PARTS):
+            passing_right(part).wait_send()
+        passing_first().wait_send()
+        passing_env().wait_send()
 
 
 def per_device(segs, sectors, psi, left_env, right_env, term_kind, block_rows):
     _, blk, cols = psi.shape
     width = left_env.shape[1]
+    ahead = min(AHEAD, width - 2)
     anywhere = pl.BlockSpec(memory_space=pl.ANY)
     result = pl.pallas_call(
         functools.partial(kernel, segs, sectors),
@@ -348,8 +372,10 @@
             pltpu.VMEM((6, 5, blk, cols), jnp.bfloat16),
             pltpu.VMEM((5, blk, cols), jnp.bfloat16),
             pltpu.VMEM((KRYLOV + 1, blk, cols), jnp.float32),
-            pltpu.VMEM((width, blk, blk), jnp.bfloat16),
-            pltpu.VMEM((width, blk, blk), jnp.bfloat16),
+            pltpu.VMEM((ahead, cols, cols), jnp.bfloat16),
+            pltpu.VMEM((blk, cols), jnp.bfloat16),
+            pltpu.VMEM((width - ahead, blk, blk), jnp.bfloat16),
+            pltpu.VMEM((width - ahead, blk, blk), jnp.bfloat16),
             pltpu.VMEM((16, 128), jnp.float32),
             pltpu.VMEM((2, sectors, 128), jnp.float32),
             pltpu.SemaphoreType.DMA((5,)),
@@ -357,6 +383,8 @@
             pltpu.SemaphoreType.DMA((6, 5)),
             pltpu.SemaphoreType.DMA((2,)),
             pltpu.SemaphoreType.DMA((2,)),
+            pltpu.SemaphoreType.DMA((AHEAD_PARTS,)),
+            pltpu.SemaphoreType.DMA((AHEAD_PARTS,)),
             pltpu.SemaphoreType.DMA((2,)),
             pltpu.SemaphoreType.DMA((2,)),
             pltpu.SemaphoreType.REGULAR((3,)),

time: 79 us -> 71.1 us (0.90)
  Pallas kernels: 76 us -> 68.5 us
    pallas_call x1, Pallas kernels: 76 us -> 68.5 us  [per_device(): pl.pallas_call(functools.partial(kernel, segs, sectors), out_shape=jax.Sh...]
where the time goes in v3:
time: 71.1 us; the launch traced here: 70.7 us
  Pallas kernels  68.5 us (96%)
  local copies, waits for them, and re-layouts  1.57 us (2%)
    pallas_call x1, Pallas kernels, per_device(): pl.pallas_call(functools.partial(kernel, segs, sectors), out_shape=jax.Sh...  68.5 us
    unnamed x1, local copies, waits for them, and re-layouts  1.57 us

profile of v3, /device:TPU:6, one launch (start us, length us, event | category | flops | bytes accessed | tf_op | source)
XLA Modules:
  0.0 70.7 jit_solution(15456149253705026694)
XLA Ops:
  0.7 68.5 %shard_map.55 = f32[128,256]{1,0:T(8,128)} custom-call(s32[26]{0:T(128)} %kinds_in.1, s32[1,1]{1,0:T(1,128)S(6)} %copy.7.rows_in, f32[128,256]{1,0:T(8,128)} %bitcast.7, bf16[26,128,128]{2,1,0:T(8,128)(2,1)} %bitcast.5, bf16[26,256,256]{2,1,0:T(8,128)(2,1)} %bitcast.4), custom_call_target="tpu_custom_call" | custom-call | tf_op jit(solution)/shard_map/pallas_call | solution.py:360
  69.1 1.6 %copy.8 = f32[1,128,256]{2,1,0:T(8,128)} copy(f32[1,128,256]{2,1,0:T(8,128)} %bitcast.6) | data formatting | bytes 262144

commit v4 on v3

--- a/solution.py
+++ b/solution.py
@@ -76,9 +76,10 @@
 
 def kernel(
     segs, sectors, kinds_in, rows_in, psi, left, right, out,
-    kinds, rows, start_v, r_v, l_v, z_v, src, chosen, u, r_prev, first_prev, env_out, env_in, table, red,
+    kinds, rows, start_v, r_v, l_v, z_v, src_0, src_1, src_2, src_3, src_4, src_5, u, r_prev, first_prev, env_out, env_in, table, red,
     load_sem, ex_send, ex_recv, red_send, red_recv, ahead_send, ahead_recv, env_send, env_recv, hello,
 ):
+    src = (src_0, src_1, src_2, src_3, src_4, src_5)
     width, blk, cols = l_v.shape[0], l_v.shape[1], r_v.shape[2]
     grid_rows = sectors // NDN
     seg, sec = lax.axis_index("seg"), lax.axis_index("sec")
@@ -87,6 +88,9 @@
 
     def beside(rows_on):
         return (seg, lax.rem(row + rows_on + grid_rows, grid_rows) * NDN + col)
+
+    def along(columns_on):
+        return (seg, row * NDN + lax.rem(col + columns_on + NDN, NDN))
 
     loads = [
         pltpu.make_async_copy(psi, start_v, load_sem.at[0]),
@@ -99,11 +103,9 @@
     loads[1].start()
 
     barrier = pltpu.get_barrier_semaphore()
-    for rows_on in (-1, 1):
-        pl.semaphore_signal(barrier, inc=1, device_id=beside(rows_on), device_id_type=MESH)
-    for j in range(1, NDN):
-        other = row * NDN + lax.rem(col + j, NDN)
-        pl.semaphore_signal(barrier, inc=1, device_id=(seg, other), device_id_type=MESH)
+    for on in (-1, 1):
+        pl.semaphore_signal(barrier, inc=1, device_id=beside(on), device_id_type=MESH)
+        pl.semaphore_signal(barrier, inc=1, device_id=along(on), device_id_type=MESH)
     before = lax.rem(seg + segs - 1, segs)
     pl.semaphore_signal(barrier, inc=1, device_id=(before, sec), device_id_type=MESH)
 
@@ -113,22 +115,22 @@
     loads[1].wait()
     live = lax.broadcasted_iota(jnp.int32, (blk, cols), 0) < rows[0, 0]
     start = jnp.where(live, start_v[...], 0.0)
-    src[0, 0] = start.astype(jnp.bfloat16)
-
-    pl.semaphore_wait(barrier, 2 + NDN - 1 + 1)
+    src[0][0] = start.astype(jnp.bfloat16)
+
+    pl.semaphore_wait(barrier, 4 + 1)
 
     neighbours = (
+        (1, 1, col < NDN - 1),
+        (2, -1, col > 0),
         (3, NDN, row < grid_rows - 1),
         (4, -NDN, row > 0),
-        (1, 1, col < NDN - 1),
-        (2, -1, col > 0),
     )
     mirrored = {1: col > 0, 2: col < NDN - 1, 3: row > 0, 4: row < grid_rows - 1}
 
     def sending(step, kind, offset):
         return pltpu.make_async_remote_copy(
-            src_ref=src.at[step, 0],
-            dst_ref=src.at[step, kind],
+            src_ref=src[step].at[0],
+            dst_ref=src[step].at[kind],
             send_sem=ex_send.at[step, kind],
             recv_sem=ex_recv.at[step, kind],
             device_id=(seg, sec - offset),
@@ -156,19 +158,26 @@
             def _():
                 sending(step, kind, offset).wait_send()
 
-    strides = (1, 2, 1)
+    rounds = ((1, True), (2, True), (1, False), (2, False), (1, False))
 
     def hello_start(turn):
-        for rows_on in (-strides[turn], strides[turn]):
-            pl.semaphore_signal(hello.at[turn], inc=1, device_id=beside(rows_on), device_id_type=MESH)
+        stride, both = rounds[turn]
+        for on in (-stride, stride):
+            pl.semaphore_signal(hello.at[turn], inc=1, device_id=beside(on), device_id_type=MESH)
+            if both:
+                pl.semaphore_signal(hello.at[turn], inc=1, device_id=along(on), device_id_type=MESH)
 
     def hello_wait(turn):
-        pl.semaphore_wait(hello.at[turn], 2)
+        pl.semaphore_wait(hello.at[turn], 4 if rounds[turn][1] else 2)
+
+    def hello_next(turn):
+        hello_wait(turn)
+        if turn + 1 < len(rounds):
+            hello_start(turn + 1)
 
     def right_side(step):
-        chosen[...] = src[step]
         for w in range(width):
-            source = chosen[kinds[w]]
+            source = src[step][kinds[w]]
             z_v[w * blk : (w + 1) * blk, :] = jnp.dot(
                 source, r_v[w], preferred_element_type=jnp.float32
             ).astype(jnp.bfloat16)
@@ -242,7 +251,7 @@
 
     def passing_first():
         return pltpu.make_async_remote_copy(
-            src_ref=src.at[3, 0], dst_ref=first_prev, send_sem=env_send.at[0], recv_sem=env_recv.at[0],
+            src_ref=src[3].at[0], dst_ref=first_prev, send_sem=env_send.at[0], recv_sem=env_recv.at[0],
             device_id=following, device_id_type=MESH,
         )
 
@@ -273,21 +282,20 @@
         @pl.when(jnp.logical_not(there))
         def _():
             for step in (0, 1, 2, 4, 5):
-                src[step, kind] = jnp.zeros((blk, cols), jnp.bfloat16)
+                src[step][kind] = jnp.zeros((blk, cols), jnp.bfloat16)
 
     for load in loads[2:]:
         load.wait()
 
     for step in range(KRYLOV):
+        hello_next(2 * step)
         exchange_wait(step)
-        hello_wait(step)
-        if step + 1 < KRYLOV:
-            hello_start(step + 1)
         right_side(step)
         image = left_side()
         if step + 1 < KRYLOV:
-            src[step + 1, 0] = image.astype(jnp.bfloat16)
+            src[step + 1][0] = image.astype(jnp.bfloat16)
             exchange_start(step + 1)
+            hello_next(2 * step + 1)
         u[step + 1] = image
         products(step + 1)
 
@@ -295,7 +303,7 @@
     first = mix[0] * u[0] + mix[1] * u[1] + mix[2] * u[2]
     first_bf = first.astype(jnp.bfloat16)
 
-    src[3, 0] = first_bf
+    src[3][0] = first_bf
 
     @pl.when(seg < segs - 1)
     def _():
@@ -305,10 +313,10 @@
         passing_env().start()
 
     for kind in range(1, 5):
-        mixed = mix[0] * src[0, kind].astype(jnp.float32)
-        mixed = mixed + mix[1] * src[1, kind].astype(jnp.float32)
-        mixed = mixed + mix[2] * src[2, kind].astype(jnp.float32)
-        src[3, kind] = mixed.astype(jnp.bfloat16)
+        mixed = mix[0] * src[0][kind].astype(jnp.float32)
+        mixed = mixed + mix[1] * src[1][kind].astype(jnp.float32)
+        mixed = mixed + mix[2] * src[2][kind].astype(jnp.float32)
+        src[3][kind] = mixed.astype(jnp.bfloat16)
     u[0] = first
     right_side(3)
     products(0)
@@ -333,7 +341,7 @@
             right_side(step + 3)
         image = left_side()
         if step + 1 < KRYLOV:
-            src[step + 4, 0] = image.astype(jnp.bfloat16)
+            src[step + 4][0] = image.astype(jnp.bfloat16)
             exchange_start(step + 4)
         u[step + 1] = image
         products(step + 1)
@@ -356,10 +364,10 @@
     _, blk, cols = psi.shape
     width = left_env.shape[1]
     ahead = min(AHEAD, width - 2)
-    anywhere = pl.BlockSpec(memory_space=pl.ANY)
+    anywhere = pl.BlockSpec(memory_space=pltpu.HBM)
     result = pl.pallas_call(
         functools.partial(kernel, segs, sectors),
-        out_shape=jax.ShapeDtypeStruct((blk, cols), jnp.float32),
+        out_shape=pltpu.VMEM((blk, cols), jnp.float32),
         in_specs=[anywhere] * 5,
         out_specs=pl.BlockSpec(memory_space=pltpu.VMEM),
         scratch_shapes=[
@@ -369,8 +377,7 @@
             pltpu.VMEM((width, cols, cols), jnp.bfloat16),
             pltpu.VMEM((width, blk, blk), jnp.bfloat16),
             pltpu.VMEM((width * blk, cols), jnp.bfloat16),
-            pltpu.VMEM((6, 5, blk, cols), jnp.bfloat16),
-            pltpu.VMEM((5, blk, cols), jnp.bfloat16),
+            *[pltpu.VMEM((5, blk, cols), jnp.bfloat16) for _ in range(6)],
             pltpu.VMEM((KRYLOV + 1, blk, cols), jnp.float32),
             pltpu.VMEM((ahead, cols, cols), jnp.bfloat16),
             pltpu.VMEM((blk, cols), jnp.bfloat16),
@@ -387,7 +394,7 @@
             pltpu.SemaphoreType.DMA((AHEAD_PARTS,)),
             pltpu.SemaphoreType.DMA((2,)),
             pltpu.SemaphoreType.DMA((2,)),
-            pltpu.SemaphoreType.REGULAR((3,)),
+            pltpu.SemaphoreType.REGULAR((5,)),
         ],
         compiler_params=pltpu.CompilerParams(
             collective_id=0, has_side_effects=True, vmem_limit_bytes=VMEM_LIMIT

time: 71.1 us -> 69.2 us (0.973)
  Pallas kernels: 68.5 us -> 67.5 us
  local copies, waits for them, and re-layouts: 1.57 us -> 0.66 us
    pallas_call x1, Pallas kernels: 68.5 us -> 67.5 us  [per_device(): pl.pallas_call(functools.partial(kernel, segs, sectors), out_shape=pltpu....]
    unnamed x1, local copies, waits for them, and re-layouts: 1.57 us -> 0.66 us
where the time goes in v4:
time: 69.2 us; the launch traced here: 68.9 us
  Pallas kernels  67.5 us (98%)
    pallas_call x1, Pallas kernels, per_device(): pl.pallas_call(functools.partial(kernel, segs, sectors), out_shape=pltpu....  67.5 us

profile of v4, /device:TPU:6, one launch (start us, length us, event | category | flops | bytes accessed | tf_op | source)
XLA Modules:
  0.0 68.9 jit_solution(12540380786715419537)
XLA Ops:
  0.7 67.5 %shard_map.55 = f32[128,256]{1,0:T(8,128)S(1)} custom-call(s32[26]{0:T(128)} %kinds_in.1, s32[1,1]{1,0:T(1,128)S(6)} %copy.8.rows_in, f32[128,256]{1,0:T(8,128)} %bitcast.7, bf16[26,128,128]{2,1,0:T(8,128)(2,1)} %bitcast.6, bf16[26,256,256]{2,1,0:T(8,128)(2,1)} %bitcast.5), custom_call_target="tpu_custom_call" | custom-call | tf_op jit(solution)/shard_map/pallas_call | solution.py:368
  68.2 0.7 copy.7

commit v5 on v4

--- a/solution.py
+++ b/solution.py
@@ -137,10 +137,17 @@
             device_id_type=MESH,
         )
 
+    low, high = NDN // 2 - 1, NDN // 2
+    inside = {1: jnp.logical_and(col > 0, col != high), 2: jnp.logical_and(col < NDN - 1, col != low)}
+
     def exchange_start(step):
-        for kind, offset, _ in neighbours:
-
-            @pl.when(mirrored[kind])
+        order = (
+            (1, 1, col == high), (2, -1, col == low), (3, NDN, mirrored[3]), (4, -NDN, mirrored[4]),
+            (1, 1, inside[1]), (2, -1, inside[2]),
+        )
+        for kind, offset, there in order:
+
+            @pl.when(there)
             def _():
                 sending(step, kind, offset).start()
 

time: 69.2 us -> 69.2 us (level)
  no operation moved by 1% of the time
where the time goes in v5:
time: 69.2 us; the launch traced here: 68.9 us
  Pallas kernels  67.6 us (98%)
    pallas_call x1, Pallas kernels, per_device(): pl.pallas_call(functools.partial(kernel, segs, sectors), out_shape=pltpu....  67.6 us

profile of v5, /device:TPU:6, one launch (start us, length us, event | category | flops | bytes accessed | tf_op | source)
XLA Modules:
  0.0 68.9 jit_solution(15172377885391261486)
XLA Ops:
  0.7 67.6 %shard_map.55 = f32[128,256]{1,0:T(8,128)S(1)} custom-call(s32[26]{0:T(128)} %kinds_in.1, s32[1,1]{1,0:T(1,128)S(6)} %copy.8.rows_in, f32[128,256]{1,0:T(8,128)} %bitcast.7, bf16[26,128,128]{2,1,0:T(8,128)(2,1)} %bitcast.6, bf16[26,256,256]{2,1,0:T(8,128)(2,1)} %bitcast.5), custom_call_target="tpu_custom_call" | custom-call | tf_op jit(solution)/shard_map/pallas_call | solution.py:375
  68.2 0.7 copy.7
